TPU v7x, 32 devices: a whole 2x2x4 slice. The times are simulated.
32 devices in a mesh: pole: 2 (over y), row: 16 (over z, x, core).
Axes of the slice: x: 2, y: 2, z: 4, core: 2. Of those that a mesh axis runs over, the one named last changes fastest.
Arguments:
- root_inverse: bfloat16 [6144, 3072], P(('pole', 'row')), parts along dimension 0, may hold values from -6 to 6
- structure: int32 [16, 8], P('row'), may hold values from 0 to 11, all different within a row
- lower_panel: bfloat16 [32, 2048, 1024], P(('pole', 'row')), parts along dimension 0, may hold values from -0.125 to 0.125
- diag_inverse: bfloat16 [32, 1024, 1024], P(('pole', 'row')), parts along dimension 0, may hold values from -6 to 6
Outputs:
- inverse_off: bfloat16 [32, 2048, 1024], P(('pole', 'row')), parts along dimension 0
- inverse_diag: bfloat16 [32, 1024, 1024], P(('pole', 'row')), parts along dimension 0
There are 2 independent parts, one for each index of `pole`. A program takes and returns all parts, laid end to end along the dimension named above; an argument that names none is the same for every part. Nothing has to cross between parts.
Inputs may be any that keep to these rules, and one draw needn't show every extreme that they name: `structure`: the 8 root blocks named by one child are distinct; every root block is named by some child.
All inputs are finite; a program needn't handle non-finite values.
Results may differ from a plain program's by a relative error of at most 0.0041.
Values may be sent and summed in bfloat16 or wider, within the bound.
A program may use at most 128 MiB of HBM per device.

v0:
```python
import jax
import jax.numpy as jnp
from jax import lax
from jax.sharding import PartitionSpec as P

B = 256
RB = 12
S = 8


def per_device(root_inverse, structure, lower_panel, diag_inverse):
    owned = structure.shape[0]
    rows_here = root_inverse.shape[0]
    row_slab = root_inverse.reshape(rows_here, RB, B)
    all_ids = lax.all_gather(structure, "row", axis=0, tiled=True)
    outgoing = jnp.take(row_slab, all_ids.reshape(-1), axis=1)
    outgoing = outgoing.reshape(rows_here, lax.axis_size("row"), owned, S * B)
    incoming = lax.all_to_all(outgoing, "row", split_axis=1, concat_axis=0, tiled=True)
    whole_cols = incoming.reshape(RB, B, owned, S * B)
    child = 0
    root_block = jnp.take(whole_cols[:, :, child], structure[child], axis=0).reshape(S * B, S * B)
    products = [jnp.dot(root_block, lower_panel[child], preferred_element_type=jnp.float32)]
    child = 0
    off_block = (-products[child]).astype(jnp.bfloat16)
    update = lax.dot_general(
        lower_panel[child], off_block, (((0,), (0,)), ((), ())), preferred_element_type=jnp.float32
    )
    diag_block = (diag_inverse[child].astype(jnp.float32) - update).astype(jnp.bfloat16)
    off_list = [off_block]
    diag_list = [diag_block]
    return (jnp.stack(off_list), jnp.stack(diag_list))


def solution(mesh):
    in_specs = (
        P(("pole", "row"), None),
        P("row", None),
        P(("pole", "row"), None, None),
        P(("pole", "row"), None, None),
    )
    out_specs = (P(("pole", "row"), None, None), P(("pole", "row"), None, None))
    return jax.shard_map(
        per_device, mesh=mesh, in_specs=in_specs, out_specs=out_specs, check_vma=False
    )
```

profile of v0, /device:TPU:11, one launch (start us, length us, event | category | flops | bytes accessed | tf_op | source)
XLA Modules:
  0.0 408.2 jit_solution(8242324789767015228)
XLA Ops:
  0.6 15.7 %all-gather = s32[16,1,8]{2,1,0:T(1,128)S(1)} all-gather(s32[1,1,8]{2,1,0:T(1,128)} %bitcast.51), channel_id=1, replica_groups=mesh['pole'=2,'row'=16] {'row'}, dimensions={0}, use_global_device_ids=true | all-gather | bytes 544 | tf_op jit(solution)/shard_map/all_gather | solution.py:15
  16.3 0.1 copy.22
  16.4 0.5 broadcast.122
  16.9 0.7 reduce.3
  17.5 0.1 reshape.134
  17.7 1.4 copy.32
  19.0 8.3 %gather_fusion = bf16[128,192,256]{2,1,0:T(8,128)(2,1)} fusion(bf16[192,12,256]{2,0,1:T(8,128)(2,1)S(1)} %bitcast.45, s32[1024]{0:T(1024)S(1)} %pad_clamp_fusion.1), kind=kCustom, calls=%fused_computation | custom fusion | bytes 25166336 | tf_op jit(solution)/shard_map/jit(_take)/gather | solution.py:16
  27.3 14.0 %copy.25 = bf16[192,128,256]{2,1,0:T(8,128)(2,1)} copy(bf16[192,128,256]{2,0,1:T(8,128)(2,1)} %bitcast.46) | data formatting | bytes 25165824 | tf_op jit(solution)/shard_map/jit(_take)/gather | solution.py:16
  41.3 19.5 %gather.11 = bf16[192,16,1,2048]{3,1,0,2:T(8,128)(2,1)} reshape(bf16[192,128,256]{2,1,0:T(8,128)(2,1)} %copy.25) | data formatting | bytes 25165824 | tf_op jit(solution)/shard_map/jit(_take)/gather | solution.py:16
  60.9 0.1 copy.23
  61.0 0.1 broadcast_in_dim.25
  61.1 6.3 %broadcast_select_fusion = bf16[192,16,1,2048]{3,1,0,2:T(8,128)(2,1)S(1)} fusion(bf16[192,16,1,2048]{3,1,0,2:T(8,128)(2,1)} %gather.11, pred[16,2048]{1,0:T(8,128)(4,1)S(1)} %bitcast.49), kind=kLoop, calls=%fused_computation.2 | loop fusion | flops 6291456 | bytes 25198592 | tf_op jit(solution)/shard_map/jit(_take)/select_n | solution.py:16
  67.4 18.3 %copy.26 = bf16[192,16,1,2048]{3,0,2,1:T(8,128)(2,1)} copy(bf16[192,16,1,2048]{3,1,0,2:T(8,128)(2,1)S(1)} %broadcast_select_fusion) | data formatting | bytes 25165824 | tf_op jit(solution)/shard_map/jit(_take)/select_n | solution.py:16
  85.7 0.0 copy-start
  85.7 0.0 copy-start.2
  85.7 11.6 %all-to-all-start = ((bf16[192,16,1,2048]{3,0,2,1:T(8,128)(2,1)}), bf16[192,16,1,2048]{3,0,2,1:T(8,128)(2,1)}, u32[]{:S(2)}, u32[]{:S(2)}) async-start(bf16[192,16,1,2048]{3,0,2,1:T(8,128)(2,1)} %copy.26), calls=%async_computation | async-start | bytes 25165824 | tf_op jit(solution)/shard_map/all_to_all | solution.py:18
  97.3 0.0 copy-done
  97.3 2.6 copy.27
  99.9 0.0 copy-done.2
  99.9 269.7 %all-to-all-done = bf16[192,16,1,2048]{3,0,2,1:T(8,128)(2,1)} async-done(((bf16[192,16,1,2048]{3,0,2,1:T(8,128)(2,1)}), bf16[192,16,1,2048]{3,0,2,1:T(8,128)(2,1)}, u32[]{:S(2)}, u32[]{:S(2)}) %all-to-all-start) | async-done | bytes 12582944 | tf_op jit(solution)/shard_map/all_to_all | solution.py:18
  369.6 9.2 %gather_fusion.1 = bf16[8,256,2048]{2,1,0:T(8,128)(2,1)} fusion(bf16[12,256,2048]{2,1,0:T(8,128)(2,1)} %bitcast.7, s32[1024]{0:T(1024)S(1)} %pad_clamp_fusion), kind=kCustom, calls=%fused_computation.1 | custom fusion | bytes 16777248 | tf_op jit(solution)/shard_map/jit(_take)/gather | solution.py:21
  378.8 7.4 %broadcast_select_fusion.1 = bf16[8,256,2048]{2,1,0:T(8,128)(2,1)} fusion(bf16[8,256,2048]{2,1,0:T(8,128)(2,1)} %gather_fusion.1, pred[8]{0:T(512)(128)(4,1)S(1)} %compare_and_fusion.1), kind=kLoop, calls=%fused_computation.4 | loop fusion | flops 4194304 | bytes 16777224 | tf_op jit(solution)/shard_map/jit(_take)/select_n | solution.py:21
  386.3 0.0 copy-start.1
  386.3 0.0 copy-start.3
  386.3 12.6 %negate_convert_fusion = bf16[2048,1024]{1,0:T(8,128)(2,1)S(1)} fusion(bf16[2048,2048]{1,0:T(8,128)(2,1)} %bitcast.47, bf16[1,2048,1024]{2,1,0:T(8,128)(2,1)} %param.6), kind=kOutput, calls=%fused_computation.3 | convolution fusion | flops 8594128896 | bytes 16777216 | tf_op jit(solution)/shard_map/dot_general | solution.py:22
  398.9 0.0 copy-start.4
  398.9 2.0 copy-done.4
  400.9 0.0 copy-done.1
  400.9 0.0 copy-done.3
  400.9 4.8 %fusion.4 = bf16[1,1024,1024]{1,2,0:T(8,128)(2,1)S(1)} fusion(bf16[1,1024,1024]{1,2,0:T(8,128)(2,1)S(1)} %copy-done.1, bf16[2048,1024]{1,0:T(8,128)(2,1)S(1)} %negate_convert_fusion, bf16[1,2048,1024]{2,1,0:T(8,128)(2,1)S(1)} %copy-done.3), kind=kOutput, calls=%fused_computation.10 | convolution fusion | flops 4298113024 | bytes 12582912 | tf_op jit(solution)/shard_map/dot_general | solution.py:25
  405.7 2.6 copy.28
  (7 shorter events, 0.1 us)
Async XLA Ops:
  85.7 11.6 %copy-start = (bf16[1,1024,1024]{2,1,0:T(8,128)(2,1)S(1)}, bf16[1,1024,1024]{2,1,0:T(8,128)(2,1)}, u32[]{:S(2)}) copy-start(bf16[1,1024,1024]{2,1,0:T(8,128)(2,1)} %param.7) | copy-start | bytes 6291460
  85.7 14.2 %copy-start.2 = (s32[1,8]{1,0:T(1,128)S(1)}, s32[1,8]{1,0:T(1,128)}, u32[]{:S(2)}) copy-start(s32[1,8]{1,0:T(1,128)} %param.5) | copy-start | bytes 100
  85.7 283.9 %all-to-all-start = ((bf16[192,16,1,2048]{3,0,2,1:T(8,128)(2,1)}), bf16[192,16,1,2048]{3,0,2,1:T(8,128)(2,1)}, u32[]{:S(2)}, u32[]{:S(2)}) async-start(bf16[192,16,1,2048]{3,0,2,1:T(8,128)(2,1)} %copy.26), calls=%async_computation | async-start | bytes 25165824 | tf_op jit(solution)/shard_map/all_to_all | solution.py:18
  386.3 14.6 %copy-start.1 = (bf16[1,1024,1024]{1,2,0:T(8,128)(2,1)S(1)}, bf16[1,1024,1024]{1,2,0:T(8,128)(2,1)}, u32[]{:S(2)}) copy-start(bf16[1,1024,1024]{1,2,0:T(8,128)(2,1)} %copy.27) | copy-start | bytes 6291460
  386.3 14.6 %copy-start.3 = (bf16[1,2048,1024]{2,1,0:T(8,128)(2,1)S(1)}, bf16[1,2048,1024]{2,1,0:T(8,128)(2,1)}, u32[]{:S(2)}) copy-start(bf16[1,2048,1024]{2,1,0:T(8,128)(2,1)} %param.6) | copy-start | bytes 12582916
  398.9 2.0 copy-start.4
where the time goes:
time: 409 us; the launch traced here: 408 us
  waiting for transfers between devices  270 us (66%)
  local copies, waits for them, and re-layouts  78.7 us (19%)
  matrix products  17.4 us (4%)
  blocking collectives  15.7 us (4%)
  other arithmetic  14.5 us (4%)
  starting transfers between devices  11.6 us (3%)
    all_to_all x1, waiting for transfers between devices, per_device(): lax.all_to_all(outgoing, 'row', split_axis=1, concat_axis=0, tiled=True)  270 us
    gather x3, local copies, waits for them, and re-layouts, per_device(): outgoing = jnp.take(row_slab, all_ids.reshape(-1), axis=1)  41.8 us
    select_n x1, local copies, waits for them, and re-layouts, per_device(): outgoing = jnp.take(row_slab, all_ids.reshape(-1), axis=1)  18.3 us
    all_gather x1, blocking collectives, per_device(): all_ids = lax.all_gather(structure, 'row', axis=0, tiled=True)  15.7 us
    dot_general x1, matrix products, per_device(): jnp.dot(root_block, lower_panel[child], preferred_element_type=jnp.float32)  12.6 us
    all_to_all x1, starting transfers between devices, per_device(): lax.all_to_all(outgoing, 'row', split_axis=1, concat_axis=0, tiled=True)  11.6 us
    gather x1, local copies, waits for them, and re-layouts, per_device(): jnp.take(whole_cols[:, :, child], structure[child], axis=0)  9.23 us
  transfers between devices with their start and end apart: 1, of which 1 were waited for; matrix products, arithmetic and copies ran while one was open for 1% of the time, Pallas kernels for 0%

commit v1 on v0

v1 whole, which is shorter than its diff:
```python
import jax
import jax.numpy as jnp
from jax import lax
from jax.experimental import pallas as pl
from jax.experimental.pallas import tpu as pltpu
from jax.sharding import PartitionSpec as P

B = 256
RB = 12
S = 8
MESH = pl.DeviceIdType.MESH
Q = 2
SUB = 2 * Q
TILE = 256
STRIP = 16


def pick(index, values):
    out = values[-1]
    for i in range(len(values) - 2, -1, -1):
        out = jnp.where(index == i, values[i], out)
    return out


def gather_kernel(
    root, struct, lower, diag_in, off_out, diag_out,
    gbuf, lv, lfull, acc, offv, dv, lt,
    recv, send_sib, send_x, send_zp, send_zm, own_sem, in_sem, off_sem, out_sem,
):
    piece = gbuf.shape[2]
    half = piece * Q
    pole = lax.axis_index("pole")
    me = lax.axis_index("row")
    core = me % 2
    x = (me // 2) % 2
    z = me // 4
    low = z < 2
    end = jnp.logical_or(z == 0, z == 3)
    mid = jnp.logical_not(end)

    def zn(i):
        return jnp.where(low, i, 3 - i)

    ia = jnp.where(end, 0, 1)
    za, zb, z2, z3 = zn(ia), zn(1 - ia), zn(2), zn(3)
    zsym = {"a": za, "b": zb, "2": z2, "3": z3}

    def device(zz, xx, cc):
        return (pole, (zz * 2 + xx) * 2 + cc)

    peers = {
        "sib": (device(z, x, 1 - core), send_sib),
        "x": (device(z, 1 - x, core), send_x),
        "zp": (device(zb, x, core), send_zp),
        "zm": (device(z2, x, core), send_zm),
    }

    def unit_of(zz, xx, h):
        return (zz * 2 + xx) * 2 + h

    sent = []

    def copy_of(direction, name, other, c, from_input=False):
        peer, sems = peers[direction]
        h, q = c // Q, c % Q
        unit = unit_of(zsym[name], 1 - x if other else x, h)
        sub = core * Q + q
        dst = gbuf.at[unit, sub]
        src = root.at[h, q] if from_input else dst
        return pltpu.make_async_remote_copy(
            src_ref=src, dst_ref=dst,
            send_sem=sems.at[unit, q], recv_sem=recv.at[unit, sub],
            device_id=peer, device_id_type=MESH,
        )

    def forward(when, direction, name, other, c, from_input=False):
        sent.append((when, direction, name, other, c, from_input))
        copy_of(direction, name, other, c, from_input).start()

    def arrive(name, other, c):
        copy_of("sib", name, other, c).wait_recv()

    own_copies = [
        pltpu.make_async_copy(
            root.at[c // Q, c % Q],
            gbuf.at[unit_of(za, x, c // Q), core * Q + c % Q],
            own_sem.at[c],
        )
        for c in range(2 * Q)
    ]
    l_copy = pltpu.make_async_copy(lower, lv, in_sem.at[0])
    d_copy = pltpu.make_async_copy(diag_in, dv, in_sem.at[1])

    barrier = pltpu.get_barrier_semaphore()
    for direction in ("sib", "x", "zp"):
        pl.semaphore_signal(barrier, inc=1, device_id=peers[direction][0], device_id_type=MESH)

    @pl.when(mid)
    def _():
        pl.semaphore_signal(barrier, inc=1, device_id=peers["zm"][0], device_id_type=MESH)

    l_copy.start()
    for copy in own_copies:
        copy.start()
    d_copy.start()
    pl.semaphore_wait(barrier, jnp.where(mid, 4, 3))

    quarters = range(2 * Q)
    for c in quarters:
        forward(None, "zp", "a", False, c, True)
        forward(None, "x", "a", False, c, True)
        forward(None, "sib", "a", False, c, True)

    @pl.when(mid)
    def _():
        for c in quarters:
            forward("mid", "zm", "a", False, c, True)

    l_copy.wait()

    @pl.loop(0, RB)
    def _(r):
        weights = [jnp.where(struct[0, s] == r, 1.0, 0.0) for s in range(S)]

        @pl.loop(0, B // STRIP)
        def _(t):
            start = pl.multiple_of(t * STRIP, STRIP)
            total = jnp.zeros((STRIP, lv.shape[1]), jnp.float32)
            for s in range(S):
                total += weights[s] * lv[pl.ds(s * B + start, STRIP), :].astype(jnp.float32)
            to = pl.multiple_of(r * B + t * STRIP, STRIP)
            lfull[pl.ds(to, STRIP), :] = total.astype(jnp.bfloat16)

    d_copy.wait()
    acc[...] = dv[...].astype(jnp.float32)
    for copy in own_copies:
        copy.wait()

    def on(flag, actions):
        @pl.when(end if flag == "end" else mid)
        def _():
            actions()

    def step1(c):
        arrive("b", False, c)
        if c < Q:
            forward(None, "x", "b", False, c)
        forward(None, "sib", "b", False, c)
        on("mid", lambda: forward("mid", "zm", "b", False, c))
        arrive("a", True, c)
        forward(None, "sib", "a", True, c)
        if c >= Q:
            on("end", lambda: forward("end", "zp", "a", True, c))

        def middle():
            arrive("2", False, c)
            forward("mid", "zp", "2", False, c)
            forward("mid", "x", "2", False, c)
            forward("mid", "sib", "2", False, c)

        on("mid", middle)

    def step_b_first(c):
        arrive("b", True, c)
        forward(None, "sib", "b", True, c)

    def end_own(name, c):
        def actions():
            arrive(name, False, c)
            forward("end", "x", name, False, c)
            forward("end", "sib", name, False, c)

        on("end", actions)

    def mid_three(c):
        def actions():
            arrive("3", False, c)
            forward("mid", "zp", "3", False, c)
            forward("mid", "x", "3", False, c)
            forward("mid", "sib", "3", False, c)

        on("mid", actions)

    def mid_last(c):
        def actions():
            arrive("b", True, c)
            forward("mid", "sib", "b", True, c)
            forward("mid", "zp", "a", True, c)

        on("mid", actions)

    def end_last(c):
        def actions():
            arrive("b", True, c)
            forward("end", "sib", "b", True, c)

        on("end", actions)

    def other(name, c):
        arrive(name, True, c)
        forward(None, "sib", name, True, c)

    def phase(k):
        first, second = range(Q), range(Q, 2 * Q)
        if k == 1:
            for c in first:
                step1(c)
        elif k == 2:
            for c in second:
                step1(c)
        elif k == 3:
            for c in first:
                step_b_first(c)
                end_own("2", c)
                mid_three(c)
        elif k == 4:
            for c in first:
                other("2", c)
                end_own("2", c + Q)
                mid_three(c + Q)
        elif k == 5:
            for c in second:
                mid_last(c)
            for c in first:
                other("2", c + Q)
                end_own("3", c)
        elif k == 6:
            for c in first:
                other("3", c)
                end_own("3", c + Q)
        elif k == 7:
            for c in second:
                other("3", c)
                end_last(c)

    table = [
        ("a", 0, 0), ("a", 0, 1),
        ("b", 0, 0), ("a", 1, 0),
        ("b", 0, 1), ("a", 1, 1),
        ("b", 1, 0), ("2", 0, 0),
        ("2", 0, 1), ("2", 1, 0),
        ("2", 1, 1), ("3", 0, 0),
        ("3", 0, 1), ("3", 1, 0),
        ("3", 1, 1), ("b", 1, 1),
    ]

    def off_copy(unit, p):
        return pltpu.make_async_copy(
            offv.at[unit, p], off_out.at[unit // 2, p, unit % 2], off_sem.at[unit, p]
        )

    @pl.loop(0, 8)
    def _(g):
        for k in range(1, 8):
            pl.when(g == k)(lambda k=k: phase(k))

        @pl.loop(0, 2)
        def _(j):
            i = g * 2 + j
            chip_z = pick(i, [zsym[name] for name, _, _ in table])
            chip_x = pick(i, [1 - x if o else x for _, o, _ in table])
            h = pick(i, [jnp.int32(hh) for _, _, hh in table])
            unit = unit_of(chip_z, chip_x, h)
            for q in range(Q):
                sub = (1 - core) * Q + q
                pltpu.make_async_copy(
                    gbuf.at[unit, sub], gbuf.at[unit, sub], recv.at[unit, sub]
                ).wait()
            chip = unit // 2
            rows = []
            for p in range(2):
                start = pl.multiple_of(chip * (4 * half) + p * 2 * half + h * half, half)
                rows.append(lfull[pl.ds(start, half), :])
            lt[...] = jnp.concatenate(rows, axis=0).T

            @pl.loop(0, acc.shape[1] // TILE)
            def _(n):
                cols = pl.ds(pl.multiple_of(n * TILE, TILE), TILE)
                left = gbuf[unit].reshape(2 * half, gbuf.shape[3])
                part = jnp.dot(left, lfull[:, cols], preferred_element_type=jnp.float32)
                off = (-part).astype(jnp.bfloat16)
                offv[unit, 0, :, cols] = off[:half]
                offv[unit, 1, :, cols] = off[half:]
                acc[:, cols] -= jnp.dot(lt[...], off, preferred_element_type=jnp.float32)

            for p in range(2):
                off_copy(unit, p).start()

    dv[...] = acc[...].astype(jnp.bfloat16)
    out_copy = pltpu.make_async_copy(dv, diag_out, out_sem.at[0])
    out_copy.start()

    for flag in (None, "mid", "end"):
        def drain(flag=flag):
            for when, direction, name, o, c, from_input in sent:
                if when == flag:
                    copy_of(direction, name, o, c, from_input).wait_send()

        if flag is None:
            drain()
        else:
            on(flag, drain)

    @pl.loop(0, 16)
    def _(unit):
        for p in range(2):
            off_copy(unit, p).wait()

    out_copy.wait()


def pick_kernel(struct, off_ref, diag_ref, off_out, diag_out):
    off_out[...] = off_ref[...]
    diag_out[...] = diag_ref[...]


def fast(root_inverse, structure, lower_panel, diag_inverse):
    rows, width = root_inverse.shape
    depth, cols = lower_panel.shape[1:]
    piece = rows // (2 * Q)
    half = rows // 2
    chips = lax.axis_size("row") // 2
    units = 2 * chips
    bf16 = jnp.bfloat16
    dma = pltpu.SemaphoreType.DMA
    any_space = pl.BlockSpec(memory_space=pl.ANY)
    off_full, diag = pl.pallas_call(
        gather_kernel,
        out_shape=(
            jax.ShapeDtypeStruct((chips, 2, 2, half, cols), bf16),
            jax.ShapeDtypeStruct((cols, cols), bf16),
        ),
        in_specs=[any_space, pl.BlockSpec(memory_space=pltpu.SMEM), any_space, any_space],
        out_specs=(any_space, any_space),
        scratch_shapes=[
            pltpu.VMEM((units, SUB, piece, width), bf16),
            pltpu.VMEM((depth, cols), bf16),
            pltpu.VMEM((width, cols), bf16),
            pltpu.VMEM((cols, cols), jnp.float32),
            pltpu.VMEM((units, 2, half, cols), bf16),
            pltpu.VMEM((cols, cols), bf16),
            pltpu.VMEM((cols, 2 * half), bf16),
            dma((units, SUB)),
            dma((units, Q)),
            dma((units, Q)),
            dma((units, Q)),
            dma((units, Q)),
            dma((2 * Q,)),
            dma((2,)),
            dma((units, 2)),
            dma((1,)),
        ],
        compiler_params=pltpu.CompilerParams(
            collective_id=0, has_side_effects=True, vmem_limit_bytes=56 * 1024 * 1024
        ),
        cost_estimate=pl.CostEstimate(
            flops=2 * width * cols * (width + cols), bytes_accessed=20 * 2**20, transcendentals=0
        ),
    )(root_inverse.reshape(2, Q, piece, width), structure, lower_panel[0], diag_inverse[0])
    off_full = off_full.reshape(RB, B, cols)
    strip = cols // S
    off, diag = pl.pallas_call(
        pick_kernel,
        grid_spec=pltpu.PrefetchScalarGridSpec(
            num_scalar_prefetch=1,
            grid=(S,),
            in_specs=[
                pl.BlockSpec((1, B, cols), lambda s, st: (st[s], 0, 0)),
                pl.BlockSpec((strip, cols), lambda s, st: (s, 0)),
            ],
            out_specs=[
                pl.BlockSpec((1, B, cols), lambda s, st: (s, 0, 0)),
                pl.BlockSpec((strip, cols), lambda s, st: (s, 0)),
            ],
        ),
        out_shape=(
            jax.ShapeDtypeStruct((S, B, cols), bf16),
            jax.ShapeDtypeStruct((cols, cols), bf16),
        ),
    )(structure[0], off_full, diag)
    return off.reshape(1, depth, cols), diag[None]


def general(root_inverse, structure, lower_panel, diag_inverse):
    whole = lax.all_gather(root_inverse, "row", axis=0, tiled=True).reshape(RB, B, RB, B)
    offs, diags = [], []
    for child in range(structure.shape[0]):
        picked = jnp.take(whole, structure[child], axis=0)
        block = jnp.take(picked, structure[child], axis=2).reshape(S * B, S * B)
        lower = lower_panel[child]
        off = (-jnp.dot(block, lower, preferred_element_type=jnp.float32)).astype(jnp.bfloat16)
        update = lax.dot_general(
            lower, off, (((0,), (0,)), ((), ())), preferred_element_type=jnp.float32
        )
        offs.append(off)
        diags.append((diag_inverse[child].astype(jnp.float32) - update).astype(jnp.bfloat16))
    return jnp.stack(offs), jnp.stack(diags)


def solution(mesh):
    per_device = fast if mesh.shape["row"] == 16 else general
    in_specs = (
        P(("pole", "row"), None),
        P("row", None),
        P(("pole", "row"), None, None),
        P(("pole", "row"), None, None),
    )
    out_specs = (P(("pole", "row"), None, None), P(("pole", "row"), None, None))
    return jax.shard_map(
        per_device, mesh=mesh, in_specs=in_specs, out_specs=out_specs, check_vma=False
    )
```

time: 409 us -> 121 us (0.30)
  the two profiles are of different devices: /device:TPU:11 before, /device:TPU:1 now
where the time goes in v1:
time: 121 us
  Pallas kernels  120 us (99%)
    pallas_call x1, Pallas kernels, fast(): pl.pallas_call(gather_kernel, out_shape=(jax.ShapeDtypeStruct((chips, 2,...  112 us
    pallas_call x1, Pallas kernels, fast(): pl.pallas_call(pick_kernel, grid_spec=pltpu.PrefetchScalarGridSpec(num_sc...  8.39 us

profile of v1, /device:TPU:1, one launch (start us, length us, event | category | flops | bytes accessed | tf_op | source)
XLA Modules:
  0.0 120.6 jit_solution(7856688818712581658)
XLA Ops:
  0.6 111.6 %shard_map.59 = (bf16[8,2,2,96,1024]{4,3,2,1,0:T(8,128)(2,1)}, bf16[1024,1024]{1,0:T(8,128)(2,1)}) custom-call(bf16[2,2,48,3072]{3,2,1,0:T(8,128)(2,1)} %bitcast.13, s32[1,8]{1,0:T(1,128)} %struct.1, bf16[2048,1024]{1,0:T(8,128)(2,1)} %bitcast.9, bf16[1024,1024]{1,0:T(8,128)(2,1)} %bitcast.11), custom_call_target="tpu_custom_call" | custom-call | flops 25769803776 | bytes 20971520 | tf_op jit(solution)/shard_map/pallas_call | solution.py:327
  112.2 8.4 %shard_map.60 = (bf16[8,256,1024]{2,1,0:T(8,128)(2,1)}, bf16[1024,1024]{1,0:T(8,128)(2,1)}) custom-call(s32[8]{0:T(128)} %bitcast.8, bf16[12,256,1024]{2,1,0:T(8,128)(2,1)} %bitcast.7, bf16[1024,1024]{1,0:T(8,128)(2,1)} %get-tuple-element.7.diag_ref), custom_call_target="tpu_custom_call" | custom-call | tf_op jit(solution)/shard_map/pallas_call | solution.py:362

commit v2 on v1

--- a/solution.py
+++ b/solution.py
@@ -228,10 +228,12 @@
             for c in first:
                 other("3", c)
                 end_own("3", c + Q)
-        elif k == 7:
-            for c in second:
-                other("3", c)
-                end_last(c)
+
+    def last_phase(t):
+        step = Q // 2
+        for c in range(Q + t * step, Q + (t + 1) * step):
+            other("3", c)
+            end_last(c)
 
     table = [
         ("a", 0, 0), ("a", 0, 1),
@@ -244,47 +246,69 @@
         ("3", 1, 1), ("b", 1, 1),
     ]
 
-    def off_copy(unit, p):
+    def off_copy(unit, p, q):
         return pltpu.make_async_copy(
-            offv.at[unit, p], off_out.at[unit // 2, p, unit % 2], off_sem.at[unit, p]
+            offv.at[unit, p, q], off_out.at[unit // 2, p, unit % 2, q], off_sem.at[unit, p * Q + q]
         )
+
+    def entry(i):
+        chip_z = pick(i, [zsym[name] for name, _, _ in table])
+        chip_x = pick(i, [1 - x if o else x for _, o, _ in table])
+        return unit_of(chip_z, chip_x, pick(i, [jnp.int32(hh) for _, _, hh in table]))
+
+    def pieces_of(i):
+        tail = i >= len(table) - 2
+        unit = entry(i)
+        last = [entry(jnp.int32(len(table) - 2)), entry(jnp.int32(len(table) - 1))]
+        step = Q // 2
+        out = []
+        for k in range(2 * Q):
+            out.append((
+                jnp.where(tail, last[k // Q], unit),
+                jnp.where(tail, k % Q // step, k // Q),
+                jnp.where(tail, (i - (len(table) - 2)) * step + k % step, k % Q),
+            ))
+        return out
 
     @pl.loop(0, 8)
     def _(g):
-        for k in range(1, 8):
+        for k in range(1, 7):
             pl.when(g == k)(lambda k=k: phase(k))
 
         @pl.loop(0, 2)
         def _(j):
             i = g * 2 + j
-            chip_z = pick(i, [zsym[name] for name, _, _ in table])
-            chip_x = pick(i, [1 - x if o else x for _, o, _ in table])
-            h = pick(i, [jnp.int32(hh) for _, _, hh in table])
-            unit = unit_of(chip_z, chip_x, h)
-            for q in range(Q):
+            for t in range(2):
+                pl.when(i == 14 + t)(lambda t=t: last_phase(t))
+            pieces = pieces_of(i)
+            rows = []
+            for unit, p, q in pieces:
+                start = unit // 2 * (4 * half) + p * 2 * half + unit % 2 * half + q * piece
+                rows.append(lfull[pl.ds(pl.multiple_of(start, piece), piece), :])
+            lt[...] = jnp.concatenate(rows, axis=0).T
+            for k in range(Q):
+                tail = i >= 14
+                step = Q // 2
+                unit, _, q = pieces[k]
+                unit = jnp.where(tail, pieces[k // step * Q][0], unit)
+                q = jnp.where(tail, (i - 14) * step + k % step, q)
                 sub = (1 - core) * Q + q
                 pltpu.make_async_copy(
                     gbuf.at[unit, sub], gbuf.at[unit, sub], recv.at[unit, sub]
                 ).wait()
-            chip = unit // 2
-            rows = []
-            for p in range(2):
-                start = pl.multiple_of(chip * (4 * half) + p * 2 * half + h * half, half)
-                rows.append(lfull[pl.ds(start, half), :])
-            lt[...] = jnp.concatenate(rows, axis=0).T
 
             @pl.loop(0, acc.shape[1] // TILE)
             def _(n):
                 cols = pl.ds(pl.multiple_of(n * TILE, TILE), TILE)
-                left = gbuf[unit].reshape(2 * half, gbuf.shape[3])
+                left = jnp.concatenate([gbuf[unit, p * Q + q] for unit, p, q in pieces], axis=0)
                 part = jnp.dot(left, lfull[:, cols], preferred_element_type=jnp.float32)
                 off = (-part).astype(jnp.bfloat16)
-                offv[unit, 0, :, cols] = off[:half]
-                offv[unit, 1, :, cols] = off[half:]
+                for k, (unit, p, q) in enumerate(pieces):
+                    offv[unit, p, q, :, cols] = off[k * piece : (k + 1) * piece]
                 acc[:, cols] -= jnp.dot(lt[...], off, preferred_element_type=jnp.float32)
 
-            for p in range(2):
-                off_copy(unit, p).start()
+            for k, (unit, p, q) in enumerate(pieces):
+                off_copy(unit, p, q).start()
 
     dv[...] = acc[...].astype(jnp.bfloat16)
     out_copy = pltpu.make_async_copy(dv, diag_out, out_sem.at[0])
@@ -304,14 +328,27 @@
     @pl.loop(0, 16)
     def _(unit):
         for p in range(2):
-            off_copy(unit, p).wait()
+            for q in range(Q):
+                off_copy(unit, p, q).wait()
 
     out_copy.wait()
 
 
-def pick_kernel(struct, off_ref, diag_ref, off_out, diag_out):
-    off_out[...] = off_ref[...]
-    diag_out[...] = diag_ref[...]
+def pick_kernel(struct, off_ref, diag_ref, off_out, diag_out, buf, dbuf, read_sem, write_sem):
+    reads, writes = [], []
+    for i in range(2):
+        reads.append(pltpu.make_async_copy(diag_ref.at[i], dbuf.at[i], read_sem.at[i]))
+        writes.append(pltpu.make_async_copy(dbuf.at[i], diag_out.at[i], write_sem.at[i]))
+    for s in range(S):
+        reads.append(pltpu.make_async_copy(off_ref.at[struct[0, s]], buf.at[s], read_sem.at[2 + s]))
+        writes.append(pltpu.make_async_copy(buf.at[s], off_out.at[s], write_sem.at[2 + s]))
+    for copy in reads:
+        copy.start()
+    for read, write in zip(reads, writes):
+        read.wait()
+        write.start()
+    for copy in writes:
+        copy.wait()
 
 
 def fast(root_inverse, structure, lower_panel, diag_inverse):
@@ -327,7 +364,7 @@
     off_full, diag = pl.pallas_call(
         gather_kernel,
         out_shape=(
-            jax.ShapeDtypeStruct((chips, 2, 2, half, cols), bf16),
+            jax.ShapeDtypeStruct((chips, 2, 2, Q, piece, cols), bf16),
             jax.ShapeDtypeStruct((cols, cols), bf16),
         ),
         in_specs=[any_space, pl.BlockSpec(memory_space=pltpu.SMEM), any_space, any_space],
@@ -337,7 +374,7 @@
             pltpu.VMEM((depth, cols), bf16),
             pltpu.VMEM((width, cols), bf16),
             pltpu.VMEM((cols, cols), jnp.float32),
-            pltpu.VMEM((units, 2, half, cols), bf16),
+            pltpu.VMEM((units, 2, Q, piece, cols), bf16),
             pltpu.VMEM((cols, cols), bf16),
             pltpu.VMEM((cols, 2 * half), bf16),
             dma((units, SUB)),
@@ -347,7 +384,7 @@
             dma((units, Q)),
             dma((2 * Q,)),
             dma((2,)),
-            dma((units, 2)),
+            dma((units, SUB)),
             dma((1,)),
         ],
         compiler_params=pltpu.CompilerParams(
@@ -358,27 +395,23 @@
         ),
     )(root_inverse.reshape(2, Q, piece, width), structure, lower_panel[0], diag_inverse[0])
     off_full = off_full.reshape(RB, B, cols)
-    strip = cols // S
     off, diag = pl.pallas_call(
         pick_kernel,
-        grid_spec=pltpu.PrefetchScalarGridSpec(
-            num_scalar_prefetch=1,
-            grid=(S,),
-            in_specs=[
-                pl.BlockSpec((1, B, cols), lambda s, st: (st[s], 0, 0)),
-                pl.BlockSpec((strip, cols), lambda s, st: (s, 0)),
-            ],
-            out_specs=[
-                pl.BlockSpec((1, B, cols), lambda s, st: (s, 0, 0)),
-                pl.BlockSpec((strip, cols), lambda s, st: (s, 0)),
-            ],
-        ),
         out_shape=(
             jax.ShapeDtypeStruct((S, B, cols), bf16),
-            jax.ShapeDtypeStruct((cols, cols), bf16),
+            jax.ShapeDtypeStruct((2, cols // 2, cols), bf16),
         ),
-    )(structure[0], off_full, diag)
-    return off.reshape(1, depth, cols), diag[None]
+        in_specs=[pl.BlockSpec(memory_space=pltpu.SMEM), any_space, any_space],
+        out_specs=(any_space, any_space),
+        scratch_shapes=[
+            pltpu.VMEM((S, B, cols), bf16),
+            pltpu.VMEM((2, cols // 2, cols), bf16),
+            dma((S + 2,)),
+            dma((S + 2,)),
+        ],
+        compiler_params=pltpu.CompilerParams(vmem_limit_bytes=60 * 1024 * 1024),
+    )(structure, off_full, diag.reshape(2, cols // 2, cols))
+    return off.reshape(1, depth, cols), diag.reshape(1, cols, cols)
 
 
 def general(root_inverse, structure, lower_panel, diag_inverse):

time: 121 us -> 118 us (0.975)
  Pallas kernels: 120 us -> 118 us
    pallas_call x1, Pallas kernels: 8.39 us -> 5.99 us  [fast(): pl.pallas_call(pick_kernel, out_shape=(jax.ShapeDtypeStruct((S, B, cols),...]
where the time goes in v2:
time: 118 us
  Pallas kernels  118 us (100%)
    pallas_call x1, Pallas kernels, fast(): pl.pallas_call(gather_kernel, out_shape=(jax.ShapeDtypeStruct((chips, 2,...  112 us
    pallas_call x1, Pallas kernels, fast(): pl.pallas_call(pick_kernel, out_shape=(jax.ShapeDtypeStruct((S, B, cols),...  5.99 us

profile of v2, /device:TPU:1, one launch (start us, length us, event | category | flops | bytes accessed | tf_op | source)
XLA Modules:
  0.0 118.3 jit_solution(17501045318224833142)
XLA Ops:
  0.6 111.7 %shard_map.59 = (bf16[8,2,2,2,48,1024]{5,4,3,2,1,0:T(8,128)(2,1)}, bf16[1024,1024]{1,0:T(8,128)(2,1)}) custom-call(bf16[2,2,48,3072]{3,2,1,0:T(8,128)(2,1)} %bitcast.13, s32[1,8]{1,0:T(1,128)} %struct.3, bf16[2048,1024]{1,0:T(8,128)(2,1)} %bitcast.9, bf16[1024,1024]{1,0:T(8,128)(2,1)} %bitcast.11), custom_call_target="tpu_custom_call" | custom-call | flops 25769803776 | bytes 20971520 | tf_op jit(solution)/shard_map/pallas_call | solution.py:364
  112.3 6.0 %shard_map.60 = (bf16[8,256,1024]{2,1,0:T(8,128)(2,1)}, bf16[2,512,1024]{2,1,0:T(8,128)(2,1)}) custom-call(s32[1,8]{1,0:T(1,128)} %struct.3, bf16[12,256,1024]{2,1,0:T(8,128)(2,1)} %bitcast.7, bf16[2,512,1024]{2,1,0:T(8,128)(2,1)} %bitcast.8), custom_call_target="tpu_custom_call" | custom-call | tf_op jit(solution)/shard_map/pallas_call | solution.py:398
